TPU v7x, 128 devices: a whole 4x4x4 slice. The times are simulated.
128 devices in a mesh: ex: 16 (over y, x), lay: 8 (over z, core).
Axes of the slice: x: 4, y: 4, z: 4, core: 2. Of those that a mesh axis runs over, the one named last changes fastest.
Arguments:
- grads: bfloat16 [8, 16384, 4096], P('lay', 'ex'), may hold values from -0.119628906 to 0.119628906
- prec_in: bfloat16 [8, 64, 64], P('lay'), as said below
- prec_out: bfloat16 [8, 64, 64], P('lay'), as said below
- requests: int32 [16, 16], replicated, may hold values from 0 to 7
- pairs: int32 [1024, 2], P('ex'), may hold values from 0 to 127, as said below
Outputs:
- gram: float32 [1024, 128, 128], P(('ex', 'lay'))
Inputs may be any that keep to these rules, and one draw needn't show every extreme that they name: Each device's listed first blocks are its own: pairs[p, 0] lies in 8 * (p // 64) to 8 * (p // 64 + 1) - 1. pairs[p, 1] is a device number of ex. The 64 pairs of one device are distinct and name every device number at least once. `prec_in`: each matrix has a diagonal between 1.5 and 6 and exceeds the sum of magnitudes of the rest of its row. `prec_out`: each matrix has a diagonal between 1.5 and 6 and exceeds the sum of magnitudes of the rest of its row.
All inputs are finite; a program needn't handle non-finite values.
Results may differ from a plain program's by a relative error of at most 0.0026.
Values may be sent and summed in bfloat16 or wider, within the bound.
No kernel may reach another device: no remote copies, remote signals or barrier semaphores. Data moves between devices by JAX's collectives and lax.ppermute only.
A program may use at most 128 MiB of HBM per device.

v0:
```python
import jax
import jax.numpy as jnp
from jax import lax
from jax.sharding import PartitionSpec as P

BLOCK = 128


def precondition(grads, prec_in, prec_out):
    layer_count, example_rows, width = grads.shape
    rank = prec_in.shape[-1]
    turned = jnp.swapaxes(grads, 1, 2).reshape(layer_count, rank, rank, example_rows)
    inner = jnp.einsum(
        "loie,lij->loje", turned, prec_in, preferred_element_type=jnp.float32
    ).astype(jnp.bfloat16)
    outer = jnp.einsum("lpo,loje->lpje", prec_out, inner, preferred_element_type=jnp.float32)
    return outer.astype(jnp.bfloat16).reshape(layer_count, width, example_rows)


def pick_tiles(products, first, source):
    return products[first, :, source, :]


def on_device(grads, prec_in, prec_out, requests, pairs):
    layer_count, example_rows, width = grads.shape
    blocks = grads.reshape(layer_count, example_rows // BLOCK, BLOCK, width)
    block_count = blocks.shape[1]
    member = lax.axis_index("ex")
    wanted = lax.dynamic_index_in_dim(requests, member, axis=1, keepdims=False)
    outgoing = jnp.take(blocks, wanted, axis=1)
    incoming = lax.all_to_all(outgoing, "ex", split_axis=1, concat_axis=1, tiled=True)
    holders = incoming.shape[1]
    left = precondition(grads, prec_in, prec_out)
    right = incoming.reshape(layer_count, holders * BLOCK, width)
    products = jnp.einsum("lqx,lmq->xm", left, right, preferred_element_type=jnp.float32)
    products = products.reshape(block_count, BLOCK, holders, BLOCK)
    first = pairs[:, 0] - member * block_count
    source = pairs[:, 1]
    pair_count = pairs.shape[0]
    share = pair_count // lax.axis_size("lay")
    terms = pick_tiles(products, first, source)
    total = lax.psum(terms, "lay")
    return lax.dynamic_slice_in_dim(total, lax.axis_index("lay") * share, share, 0)


def solution(mesh):
    placed = (P("lay", "ex", None), P("lay", None, None), P("lay", None, None), P(), P("ex", None))
    return jax.shard_map(
        on_device,
        mesh=mesh,
        in_specs=placed,
        out_specs=P(("ex", "lay"), None, None),
        check_vma=False,
    )
```

profile of v0, /device:TPU:0, one launch (start us, length us, event | category | flops | bytes accessed | tf_op | source)
XLA Modules:
  0.0 400.7 jit_solution(12002217262961592764)
XLA Ops:
  6.5 0.0 copy-start
  6.5 0.9 fusion.8
  7.4 0.9 and_reduce_fusion
  8.3 10.5 %gather_fusion = bf16[16,128,4096]{2,1,0:T(8,128)(2,1)} fusion(bf16[8,128,4096]{2,1,0:T(8,128)(2,1)} %bitcast.39, s32[1024]{0:T(1024)S(1)} %pad_clamp_fusion), kind=kCustom, calls=%fused_computation | custom fusion | bytes 33554496 | tf_op jit(solution)/shard_map/jit(_take)/gather | solution.py:30
  18.8 14.2 %bitcast_select_fusion = bf16[1,16,128,4096]{3,2,0,1:T(8,128)(2,1)} fusion(bf16[16,128,4096]{2,1,0:T(8,128)(2,1)} %gather_fusion, pred[16]{0:T(512)(128)(4,1)S(1)} %and_reduce_fusion), kind=kLoop, calls=%fused_computation.4 | loop fusion | flops 8388608 | bytes 33554448 | tf_op jit(solution)/shard_map/jit(_take)/select_n | solution.py:30
  33.0 7.2 %all-to-all-start = ((bf16[1,16,128,4096]{3,2,0,1:T(8,128)(2,1)}), bf16[1,16,128,4096]{3,2,0,1:T(8,128)(2,1)}, u32[]{:S(2)}, u32[]{:S(2)}) async-start(bf16[1,16,128,4096]{3,2,0,1:T(8,128)(2,1)} %bitcast_select_fusion), calls=%async_computation | async-start | bytes 33554432 | tf_op jit(solution)/shard_map/all_to_all | solution.py:31
  40.2 0.0 all-reduce.2.cloned.1.call-start
  40.3 12.0 %copy.14 = bf16[1,1024,4096]{1,2,0:T(8,128)(2,1)} copy(bf16[1,1024,4096]{2,1,0:T(8,128)(2,1)} %param.5) | data formatting | bytes 16777216 | tf_op args[0]
  52.2 0.0 copy-done
  52.2 0.0 copy-start.2
  52.2 5.8 %convert_bitcast_fusion.1 = bf16[64,64,1024]{2,1,0:T(8,128)(2,1)S(1)} fusion(bf16[64,64,1024]{2,1,0:T(8,128)(2,1)} %bitcast.40, bf16[1,64,64]{2,1,0:T(8,128)(2,1)S(1)} %copy-done), kind=kOutput, calls=%fused_computation.8 | convolution fusion | flops 541065216 | bytes 16785408 | tf_op jit(solution)/shard_map/loie,lij->loje/dot_general | solution.py:13
  58.0 0.0 copy-done.2
  58.0 12.9 %convert_bitcast_fusion = bf16[64,64,1024]{2,0,1:T(8,128)(2,1)} fusion(bf16[64,64,1024]{2,1,0:T(8,128)(2,1)S(1)} %convert_bitcast_fusion.1, bf16[1,64,64]{2,1,0:T(8,128)(2,1)S(1)} %copy-done.2), kind=kOutput, calls=%fused_computation.7 | convolution fusion | flops 541065216 | bytes 16785408 | tf_op jit(solution)/shard_map/lpo,loje->lpje/dot_general | solution.py:16
  70.9 11.3 %copy.17 = bf16[64,64,1024]{2,1,0:T(8,128)(2,1)} copy(bf16[64,64,1024]{2,0,1:T(8,128)(2,1)} %convert_bitcast_fusion) | data formatting | bytes 16777216 | tf_op jit(solution)/shard_map/convert_element_type | solution.py:17
  82.2 11.2 %copy.22 = bf16[1024,4096]{1,0:T(8,128)(2,1)} copy(bf16[1024,4096]{0,1:T(8,128)(2,1)} %bitcast.41) | data formatting | bytes 16777216 | tf_op jit(solution)/shard_map/lqx,lmq->xm/dot_general | solution.py:35
  93.4 0.0 copy-done.3
  93.4 196.5 %all-to-all-done = bf16[1,16,128,4096]{3,2,0,1:T(8,128)(2,1)} async-done(((bf16[1,16,128,4096]{3,2,0,1:T(8,128)(2,1)}), bf16[1,16,128,4096]{3,2,0,1:T(8,128)(2,1)}, u32[]{:S(2)}, u32[]{:S(2)}) %all-to-all-start) | async-done | bytes 16777248 | tf_op jit(solution)/shard_map/all_to_all | solution.py:31
  289.9 0.0 copy-start.1
  289.9 24.1 %fusion = f32[8,128,16,128]{3,1,2,0:T(8,128)} fusion(bf16[8,128,4096,1]{2,1,3,0:T(8,128)(2,1)} %bitcast.42, bf16[1,16,128,4096]{3,2,0,1:T(8,128)(2,1)} %all-to-all-done), kind=kOutput, calls=%fused_computation.2 | convolution fusion | flops 17179869184 | bytes 33554432 | tf_op jit(solution)/shard_map/lqx,lmq->xm/dot_general | solution.py:35
  314.0 6.1 %gather_fusion.1 = f32[64,128,128]{2,1,0:T(8,128)} fusion(f32[8,128,16,128]{3,1,2,0:T(8,128)} %fusion, s32[64]{0:T(128)S(1)} %fusion.14), kind=kCustom, calls=%fused_computation.1 | custom fusion | bytes 8389120 | tf_op jit(solution)/shard_map/gather | solution.py:21
  320.2 0.0 all-reduce.2.cloned.1.call-update
  320.2 71.8 %all-reduce.2.cloned.1.call-done = f32[64,128,128]{2,1,0:T(8,128)} async-done(((f32[64,128,128]{2,1,0:T(8,128)}), f32[64,128,128]{2,1,0:T(8,128)}) %all-reduce.2.cloned.1.call-update) | async-done | bytes 4194320 | tf_op jit(solution)/shard_map/psum | solution.py:42
  392.0 1.9 constant_dynamic-slice_fusion
  393.9 0.0 copy-done.1
  (3 shorter events, 0.0 us)
Async XLA Ops:
  6.5 45.7 %copy-start = (bf16[1,64,64]{2,1,0:T(8,128)(2,1)S(1)}, bf16[1,64,64]{2,1,0:T(8,128)(2,1)}, u32[]{:S(2)}) copy-start(bf16[1,64,64]{2,1,0:T(8,128)(2,1)} %param.6) | copy-start | bytes 24580
  33.0 257.0 %all-to-all-start = ((bf16[1,16,128,4096]{3,2,0,1:T(8,128)(2,1)}), bf16[1,16,128,4096]{3,2,0,1:T(8,128)(2,1)}, u32[]{:S(2)}, u32[]{:S(2)}) async-start(bf16[1,16,128,4096]{3,2,0,1:T(8,128)(2,1)} %bitcast_select_fusion), calls=%async_computation | async-start | bytes 33554432 | tf_op jit(solution)/shard_map/all_to_all | solution.py:31
  40.2 351.8 %all-reduce.2.cloned.1.call-start = ((), (), s32[]{:S(2)}) async-start(), calls=%async_computation.1 | async-start | bytes 8388608 | tf_op jit(solution)/shard_map/psum | solution.py:42
  52.2 5.8 %copy-start.2 = (bf16[1,64,64]{2,1,0:T(8,128)(2,1)S(1)}, bf16[1,64,64]{2,1,0:T(8,128)(2,1)}, u32[]{:S(2)}) copy-start(bf16[1,64,64]{2,1,0:T(8,128)(2,1)} %param.7) | copy-start | bytes 24580
  82.2 11.2 %copy-start.3 = (s32[64,2]{0,1:T(2,128)S(1)}, s32[64,2]{0,1:T(2,128)}, u32[]{:S(2)}) copy-start(s32[64,2]{0,1:T(2,128)} %param.9) | copy-start | bytes 1540
  289.9 103.9 %copy-start.1 = (bf16[1,64,64]{2,1,0:T(8,128)(2,1)S(1)}, bf16[1,64,64]{2,1,0:T(8,128)(2,1)}, u32[]{:S(2)}) copy-start(bf16[1,64,64]{2,1,0:T(8,128)(2,1)} %param.6) | copy-start | bytes 24580
Sparse Core Ops, SparseCore 0:
  320.3 71.6 all-reduce.1
where the time goes:
time: 402 us; the launch traced here: 401 us
  waiting for transfers between devices  268 us (67%)
  local copies, waits for them, and re-layouts  53 us (13%)
  matrix products  42.8 us (11%)
  other arithmetic  15.9 us (4%)
  between operations  13.4 us (3%)
  starting transfers between devices  7.28 us (2%)
    all_to_all x1, waiting for transfers between devices, on_device(): lax.all_to_all(outgoing, 'ex', split_axis=1, concat_axis=1, tiled=True)  197 us
    psum x1, waiting for transfers between devices, on_device(): total = lax.psum(terms, 'lay')  71.8 us
    dot_general x1, matrix products, on_device(): jnp.einsum('lqx,lmq->xm', left, right, preferred_element_type=jnp.float32)  24.1 us
    select_n x2, other arithmetic, on_device(): outgoing = jnp.take(blocks, wanted, axis=1)  15 us
    dot_general x1, matrix products, precondition(): jnp.einsum('lpo,loje->lpje', prec_out, inner, preferred_element_type=jnp....  12.9 us
    unnamed x9, local copies, waits for them, and re-layouts  12 us
    convert_element_type x1, local copies, waits for them, and re-layouts, precondition(): return outer.astype(jnp.bfloat16).reshape(layer_count, width, example_rows)  11.3 us
    dot_general x1, local copies, waits for them, and re-layouts, on_device(): jnp.einsum('lqx,lmq->xm', left, right, preferred_element_type=jnp.float32)  11.2 us
  transfers between devices with their start and end apart: 2, of which 2 were waited for; matrix products, arithmetic and copies ran while one was open for 13% of the time, Pallas kernels for 0%

commit v1 on v0

--- a/solution.py
+++ b/solution.py
@@ -2,6 +2,7 @@
 import jax.numpy as jnp
 from jax import lax
 from jax.sharding import PartitionSpec as P
+from jax.lax import all_gather
 
 BLOCK = 128
 
@@ -39,7 +40,7 @@
     pair_count = pairs.shape[0]
     share = pair_count // lax.axis_size("lay")
     terms = pick_tiles(products, first, source)
-    total = lax.psum(terms, "lay")
+    total = jnp.sum(all_gather(terms, axis_name="lay"), axis=0)
     return lax.dynamic_slice_in_dim(total, lax.axis_index("lay") * share, share, 0)
 
 

time: 402 us -> 501 us (1.25)
  waiting for transfers between devices: 268 us -> 352 us
  other arithmetic: 15.9 us -> 30.1 us
    all_gather x0 -> x1, waiting for transfers between devices: none -> 155 us  [on_device(): total = jnp.sum(all_gather(terms, axis_name='lay'), axis=0)]
    psum x1 -> x0, waiting for transfers between devices: 71.8 us -> none  [on_device(): total = lax.psum(terms, 'lay')]
    reduce_sum x0 -> x1, other arithmetic: none -> 14.2 us  [on_device(): total = jnp.sum(all_gather(terms, axis_name='lay'), axis=0)]
  transfers between devices with their start and end apart: 2 -> 2, of which waited for: 2 -> 2; matrix products, arithmetic and copies ran while one was open for 13% -> 11% of each run, Pallas kernels for 0% -> 0%
where the time goes in v1:
time: 501 us; the launch traced here: 498 us
  waiting for transfers between devices  352 us (70%)
  local copies, waits for them, and re-layouts  53.2 us (11%)
  matrix products  42.8 us (9%)
  other arithmetic  30.1 us (6%)
  between operations  13.4 us (3%)
  starting transfers between devices  7.26 us (1%)
    all_to_all x1, waiting for transfers between devices, on_device(): lax.all_to_all(outgoing, 'ex', split_axis=1, concat_axis=1, tiled=True)  197 us
    all_gather x1, waiting for transfers between devices, on_device(): total = jnp.sum(all_gather(terms, axis_name='lay'), axis=0)  155 us
    dot_general x1, matrix products, on_device(): jnp.einsum('lqx,lmq->xm', left, right, preferred_element_type=jnp.float32)  24.1 us
    select_n x2, other arithmetic, on_device(): outgoing = jnp.take(blocks, wanted, axis=1)  15 us
    reduce_sum x1, other arithmetic, on_device(): total = jnp.sum(all_gather(terms, axis_name='lay'), axis=0)  14.2 us
    dot_general x1, matrix products, precondition(): jnp.einsum('lpo,loje->lpje', prec_out, inner, preferred_element_type=jnp....  12.9 us
    unnamed x9, local copies, waits for them, and re-layouts  12 us
    convert_element_type x1, local copies, waits for them, and re-layouts, precondition(): return outer.astype(jnp.bfloat16).reshape(layer_count, width, example_rows)  11.3 us
  transfers between devices with their start and end apart: 2, of which 2 were waited for; matrix products, arithmetic and copies ran while one was open for 11% of the time, Pallas kernels for 0%

profile of v1, /device:TPU:0, one launch (start us, length us, event | category | flops | bytes accessed | tf_op | source)
XLA Modules:
  0.0 498.3 jit_solution(15924037794699853081)
XLA Ops:
  6.5 0.0 copy-start
  6.5 0.9 fusion.8
  7.4 0.9 and_reduce_fusion
  8.3 10.6 %gather_fusion = bf16[16,128,4096]{2,1,0:T(8,128)(2,1)} fusion(bf16[8,128,4096]{2,1,0:T(8,128)(2,1)} %bitcast.40, s32[1024]{0:T(1024)S(1)} %pad_clamp_fusion), kind=kCustom, calls=%fused_computation | custom fusion | bytes 33554496 | tf_op jit(solution)/shard_map/jit(_take)/gather | solution.py:31
  18.9 14.2 %bitcast_select_fusion = bf16[1,16,128,4096]{3,2,0,1:T(8,128)(2,1)} fusion(bf16[16,128,4096]{2,1,0:T(8,128)(2,1)} %gather_fusion, pred[16]{0:T(512)(128)(4,1)S(1)} %and_reduce_fusion), kind=kLoop, calls=%fused_computation.4 | loop fusion | flops 8388608 | bytes 33554448 | tf_op jit(solution)/shard_map/jit(_take)/select_n | solution.py:31
  33.1 7.2 %all-to-all-start = ((bf16[1,16,128,4096]{3,2,0,1:T(8,128)(2,1)}), bf16[1,16,128,4096]{3,2,0,1:T(8,128)(2,1)}, u32[]{:S(2)}, u32[]{:S(2)}) async-start(bf16[1,16,128,4096]{3,2,0,1:T(8,128)(2,1)} %bitcast_select_fusion), calls=%async_computation | async-start | bytes 33554432 | tf_op jit(solution)/shard_map/all_to_all | solution.py:32
  40.3 0.0 all-gather.3.cloned.1.call-start
  40.4 12.0 %copy.14 = bf16[1,1024,4096]{1,2,0:T(8,128)(2,1)} copy(bf16[1,1024,4096]{2,1,0:T(8,128)(2,1)} %param.5) | data formatting | bytes 16777216 | tf_op args[0]
  52.3 0.0 copy-done
  52.3 0.0 copy-start.2
  52.3 5.8 %convert_bitcast_fusion.1 = bf16[64,64,1024]{2,1,0:T(8,128)(2,1)S(1)} fusion(bf16[64,64,1024]{2,1,0:T(8,128)(2,1)} %bitcast.42, bf16[1,64,64]{2,1,0:T(8,128)(2,1)S(1)} %copy-done), kind=kOutput, calls=%fused_computation.8 | convolution fusion | flops 541065216 | bytes 16785408 | tf_op jit(solution)/shard_map/loie,lij->loje/dot_general | solution.py:14
  58.1 0.0 copy-done.2
  58.1 12.9 %convert_bitcast_fusion = bf16[64,64,1024]{2,0,1:T(8,128)(2,1)} fusion(bf16[64,64,1024]{2,1,0:T(8,128)(2,1)S(1)} %convert_bitcast_fusion.1, bf16[1,64,64]{2,1,0:T(8,128)(2,1)S(1)} %copy-done.2), kind=kOutput, calls=%fused_computation.7 | convolution fusion | flops 541065216 | bytes 16785408 | tf_op jit(solution)/shard_map/lpo,loje->lpje/dot_general | solution.py:17
  71.0 11.3 %copy.17 = bf16[64,64,1024]{2,1,0:T(8,128)(2,1)} copy(bf16[64,64,1024]{2,0,1:T(8,128)(2,1)} %convert_bitcast_fusion) | data formatting | bytes 16777216 | tf_op jit(solution)/shard_map/convert_element_type | solution.py:18
  82.3 11.2 %copy.22 = bf16[1024,4096]{1,0:T(8,128)(2,1)} copy(bf16[1024,4096]{0,1:T(8,128)(2,1)} %bitcast.43) | data formatting | bytes 16777216 | tf_op jit(solution)/shard_map/lqx,lmq->xm/dot_general | solution.py:36
  93.5 0.0 copy-done.3
  93.5 196.5 %all-to-all-done = bf16[1,16,128,4096]{3,2,0,1:T(8,128)(2,1)} async-done(((bf16[1,16,128,4096]{3,2,0,1:T(8,128)(2,1)}), bf16[1,16,128,4096]{3,2,0,1:T(8,128)(2,1)}, u32[]{:S(2)}, u32[]{:S(2)}) %all-to-all-start) | async-done | bytes 16777248 | tf_op jit(solution)/shard_map/all_to_all | solution.py:32
  290.0 24.1 %fusion = f32[8,128,16,128]{3,1,2,0:T(8,128)} fusion(bf16[8,128,4096,1]{2,1,3,0:T(8,128)(2,1)} %bitcast.44, bf16[1,16,128,4096]{3,2,0,1:T(8,128)(2,1)} %all-to-all-done), kind=kOutput, calls=%fused_computation.2 | convolution fusion | flops 17179869184 | bytes 33554432 | tf_op jit(solution)/shard_map/lqx,lmq->xm/dot_general | solution.py:36
  314.1 6.2 %gather_fusion.1 = f32[64,128,128]{2,1,0:T(8,128)} fusion(f32[8,128,16,128]{3,1,2,0:T(8,128)} %fusion, s32[64]{0:T(128)S(1)} %fusion.14), kind=kCustom, calls=%fused_computation.1 | custom fusion | bytes 8389120 | tf_op jit(solution)/shard_map/gather | solution.py:22
  320.4 0.0 all-gather.3.cloned.1.call-update
  320.4 155.0 %all-gather.3.cloned.1.call-done = f32[512,128,128]{2,1,0:T(8,128)} async-done(((f32[64,128,128]{2,1,0:T(8,128)}), f32[512,128,128]{2,1,0:T(8,128)}) %all-gather.3.cloned.1.call-update) | async-done | bytes 33554448 | tf_op jit(solution)/shard_map/all_gather | solution.py:43
  475.4 14.2 %reduce_sum.9 = f32[64,128,128]{2,1,0:T(8,128)} reduce(f32[8,64,128,128]{3,2,1,0:T(8,128)} %bitcast.41, f32[]{:T(128)} %constant.36.clone.1), dimensions={0}, to_apply=%region_0.1 | reduce | flops 7340032 | bytes 37748740 | tf_op jit(solution)/shard_map/reduce_sum | solution.py:43
  489.6 1.9 constant_dynamic-slice_fusion
  491.4 0.0 copy-done.1
  (4 shorter events, 0.0 us)
Async XLA Ops:
  6.5 45.8 %copy-start = (bf16[1,64,64]{2,1,0:T(8,128)(2,1)S(1)}, bf16[1,64,64]{2,1,0:T(8,128)(2,1)}, u32[]{:S(2)}) copy-start(bf16[1,64,64]{2,1,0:T(8,128)(2,1)} %param.6) | copy-start | bytes 24580
  33.1 256.9 %all-to-all-start = ((bf16[1,16,128,4096]{3,2,0,1:T(8,128)(2,1)}), bf16[1,16,128,4096]{3,2,0,1:T(8,128)(2,1)}, u32[]{:S(2)}, u32[]{:S(2)}) async-start(bf16[1,16,128,4096]{3,2,0,1:T(8,128)(2,1)} %bitcast_select_fusion), calls=%async_computation | async-start | bytes 33554432 | tf_op jit(solution)/shard_map/all_to_all | solution.py:32
  40.3 435.1 %all-gather.3.cloned.1.call-start = ((), (), s32[]{:S(2)}) async-start(), calls=%async_computation.1 | async-start | bytes 37748736 | tf_op jit(solution)/shard_map/all_gather | solution.py:43
  52.3 5.8 %copy-start.2 = (bf16[1,64,64]{2,1,0:T(8,128)(2,1)S(1)}, bf16[1,64,64]{2,1,0:T(8,128)(2,1)}, u32[]{:S(2)}) copy-start(bf16[1,64,64]{2,1,0:T(8,128)(2,1)} %param.7) | copy-start | bytes 24580
  82.3 11.2 %copy-start.3 = (s32[64,2]{0,1:T(2,128)S(1)}, s32[64,2]{0,1:T(2,128)}, u32[]{:S(2)}) copy-start(s32[64,2]{0,1:T(2,128)} %param.9) | copy-start | bytes 1540
  475.4 16.0 %copy-start.1 = (bf16[1,64,64]{2,1,0:T(8,128)(2,1)S(1)}, bf16[1,64,64]{2,1,0:T(8,128)(2,1)}, u32[]{:S(2)}) copy-start(bf16[1,64,64]{2,1,0:T(8,128)(2,1)} %param.6) | copy-start | bytes 24580
Sparse Core Ops, SparseCore 0:
  320.5 154.8 all-gather.2
